TPU v7x, 32 devices: a whole 2x2x4 slice. The times are simulated.
32 devices in a mesh: island: 2 (over y), stripe: 4 (over z), rep: 4 (over x, core).
Axes of the slice: x: 2, y: 2, z: 4, core: 2. Of those that a mesh axis runs over, the one named last changes fastest.
Arguments:
- features: bfloat16 [4096, 256], P(('island', 'stripe', 'rep')), parts along dimension 0, may hold values from -6 to 6
- tiles: bfloat16 [8, 4, 3, 128, 128], P(('island', 'stripe'), 'rep'), parts along dimension 0, as said below
- tile_row: int32 [8, 4, 3], P(('island', 'stripe'), 'rep'), parts along dimension 0, may hold values from 0 to 4, as said below
- tile_src: int32 [8, 4, 3], P(('island', 'stripe'), 'rep'), parts along dimension 0, may hold values from 0 to 3, as said below
- self_weight: bfloat16 [256, 256], replicated, may hold values from -0.375 to 0.375
- neigh_weight: bfloat16 [256, 256], replicated, may hold values from -4 to 4
- bias: bfloat16 [256], replicated, may hold values from -3 to 3
- cotangent: bfloat16 [4096, 256], P(('island', 'stripe', 'rep')), parts along dimension 0, may hold values from -6 to 6
Outputs:
- output: bfloat16 [4096, 256], P(('island', 'stripe', 'rep')), parts along dimension 0
- grad_input: float32 [4096, 256], P(('island', 'stripe', 'rep')), parts along dimension 0
- grad_self: float32 [512, 256], P('island'), parts along dimension 0
- grad_neigh: float32 [512, 256], P('island'), parts along dimension 0
- grad_bias: float32 [512], P('island'), parts along dimension 0
There are 2 independent parts, one for each index of `island`. A program takes and returns all parts, laid end to end along the dimension named above; an argument that names none is the same for every part. Nothing has to cross between parts.
Inputs may be any that keep to these rules, and one draw needn't show every extreme that they name: `tiles`: Non-negative edge weights; within a tile the nonzero share and the row scales vary. `tile_row`: value 4 marks an unused slot. Each device has a live slot for its own stripe and one for one other stripe, and for every destination stripe one device has a live slot for the stripe 4 // 2 away; all other slots are unused. A node has some 30 neighbours on average. `tile_src`: the source stripe of a slot; live slots as described for tile_row.
All inputs are finite; a program needn't handle non-finite values.
Results may differ from a plain program's by a relative error of at most 0.019.
Values may be sent and summed in bfloat16 or wider, within the bound.
A program may use at most 64 MiB of HBM per device.

v0:
```python
import jax
import jax.numpy as jnp
from jax import lax
from jax.sharding import PartitionSpec as P


def broadcast(value, axis, source):
    kept = jnp.where(lax.axis_index(axis) == source, value, 0).astype(value.dtype)
    return lax.psum(kept, axis)


def pick_blocks(row_set, count):
    return (row_set[..., None] == jnp.arange(count, dtype=jnp.int32)).astype(jnp.float32)


def shards(features, tiles, tile_row, tile_src, self_weight, neigh_weight, bias, cotangent):
    stripes = lax.axis_size("stripe")
    reps = lax.axis_size("rep")
    edge = features.shape[0]
    width = features.shape[1]
    tile_set = tiles[0, 0]
    row_set = tile_row[0, 0]
    src_set = tile_src[0, 0]
    slots = row_set.shape[0]
    onehot = pick_blocks(row_set, reps)
    row_weights = jnp.sum(tile_set, axis=-1, dtype=jnp.float32)
    degree_part = jnp.einsum("kq,ka->qa", onehot, row_weights, precision=lax.Precision.HIGHEST)

    def turn(step, slot_feats):
        block = broadcast(features, "stripe", step)
        match = (src_set == step)[:, None, None]
        return jnp.where(match, block[None], slot_feats)

    start_feats = jnp.zeros((slots, edge, width), jnp.bfloat16)
    slot_feats = lax.fori_loop(0, stripes, turn, start_feats)
    product = jnp.einsum("kab,kbf->kaf", tile_set, slot_feats, preferred_element_type=jnp.float32)
    partial_sum = jnp.einsum("kq,kaf->qaf", onehot, product, precision=lax.Precision.HIGHEST)
    agg_own, degree_own = (
        lax.psum_scatter(
            partial_sum.astype(jnp.bfloat16), "rep", scatter_dimension=0, tiled=True
        ).astype(jnp.float32),
        lax.psum_scatter(
            degree_part.astype(jnp.bfloat16), "rep", scatter_dimension=0, tiled=True
        ).astype(jnp.float32),
    )
    degree = 1.0 + degree_own[0]
    neigh = (agg_own[0] / degree[:, None]).astype(jnp.bfloat16)
    pre = (
        jnp.dot(features, self_weight, preferred_element_type=jnp.float32)
        + jnp.dot(neigh, neigh_weight, preferred_element_type=jnp.float32)
        + bias.astype(jnp.float32)
    )
    output = jax.nn.silu(pre).astype(jnp.bfloat16)
    sigma = jax.nn.sigmoid(pre)
    slope = (cotangent.astype(jnp.float32) * sigma * (1.0 + pre * (1.0 - sigma))).astype(
        jnp.bfloat16
    )
    contract_rows = (((0,), (0,)), ((), ()))
    contract_cols = (((1,), (1,)), ((), ()))
    grad_self = lax.dot_general(features, slope, contract_rows, preferred_element_type=jnp.float32)
    grad_neigh = lax.dot_general(neigh, slope, contract_rows, preferred_element_type=jnp.float32)
    grad_bias = jnp.sum(slope, axis=0, dtype=jnp.float32)
    grad_self, grad_neigh, grad_bias = lax.psum(
        (grad_self, grad_neigh, grad_bias), ("stripe", "rep")
    )
    pulled = lax.dot_general(slope, neigh_weight, contract_cols, preferred_element_type=jnp.float32)
    pull = (pulled / degree[:, None]).astype(jnp.bfloat16)
    stripe_pull = lax.all_gather(pull, "rep", axis=0, tiled=True).reshape(reps, edge, width)
    picked = jnp.einsum(
        "kq,qaf->kaf", onehot.astype(jnp.bfloat16), stripe_pull, preferred_element_type=jnp.float32
    ).astype(jnp.bfloat16)
    slot_terms = jnp.einsum("kab,kaf->kbf", tile_set, picked, preferred_element_type=jnp.float32)
    turns = edge * lax.axis_size("stripe") // edge
    wanted = jnp.arange(turns, dtype=jnp.int32)
    place = (src_set[:, None] == wanted[None, :]).astype(jnp.float32)
    term = jnp.einsum("kt,kbf->tbf", place, slot_terms, precision=lax.Precision.HIGHEST)
    spread = lax.psum_scatter(
        term.reshape(edge * lax.axis_size("stripe"), width).astype(jnp.bfloat16),
        "stripe",
        scatter_dimension=0,
        tiled=True,
    ).astype(jnp.float32)
    grad_input = (
        lax.dot_general(slope, self_weight, contract_cols, preferred_element_type=jnp.float32)
        + spread
    )
    return (output, grad_input, grad_self, grad_neigh, grad_bias)


def solution(mesh):
    return jax.shard_map(
        shards,
        mesh=mesh,
        in_specs=(
            P(("island", "stripe", "rep"), None),
            P(("island", "stripe"), "rep", None, None, None),
            P(("island", "stripe"), "rep", None),
            P(("island", "stripe"), "rep", None),
            P(),
            P(),
            P(),
            P(("island", "stripe", "rep"), None),
        ),
        out_specs=(
            P(("island", "stripe", "rep"), None),
            P(("island", "stripe", "rep"), None),
            P("island", None),
            P("island", None),
            P("island"),
        ),
        check_vma=False,
    )
```

profile of v0, /device:TPU:0, one launch (start us, length us, event | category | flops | bytes accessed | tf_op | source)
XLA Modules:
  0.0 321.4 jit_solution(1529212910113368792)
XLA Ops:
  8.0 0.7 copy-done.6
  8.7 156.2 %while.16 = (s32[]{:T(128)}, bf16[3,128,256]{2,1,0:T(8,128)(2,1)S(1)}, s32[3]{0:T(128)S(1)}, bf16[128,256]{1,0:T(8,128)(2,1)}, s32[]{:T(128)}, /*index=5*/s32[]{:T(128)}, u32[]{:T(128)}, u32[]{:T(128)}) while((s32[]{:T(128)}, bf16[3,128,256]{2,1,0:T(8,128)(2,1)S(1)}, s32[3]{0:T(128)S(1)}, bf16[128,256]{1,0:T(8,128)(2,1)}, ...), condition=%wide.region_2.0_spmd.clone, body=%wide.region_0.2_spmd.clone.sunk | while | flops 262154 | bytes 983247 | solution.py:35
  8.7 1.5 broadcast_select_fusion.2
  10.3 38.9 %all-reduce.7.cloned.1.call-done = bf16[128,256]{1,0:T(8,128)(2,1)} async-done(((bf16[128,256]{1,0:T(8,128)(2,1)}), bf16[128,256]{1,0:T(8,128)(2,1)}) %all-reduce.7.cloned.1.call-update) | async-done | bytes 65552 | tf_op jit(solution)/shard_map/while/body/eval_jaxpr/psum | solution.py:9
  49.1 0.9 select_select_fusion.2
  50.1 0.6 broadcast_select_fusion.2
  50.9 36.7 %all-reduce.7.cloned.1.call-done = bf16[128,256]{1,0:T(8,128)(2,1)} async-done(((bf16[128,256]{1,0:T(8,128)(2,1)}), bf16[128,256]{1,0:T(8,128)(2,1)}) %all-reduce.7.cloned.1.call-update) | async-done | bytes 65552 | tf_op jit(solution)/shard_map/while/body/eval_jaxpr/psum | solution.py:9
  87.5 0.9 select_select_fusion.2
  88.5 0.6 broadcast_select_fusion.2
  89.2 36.7 %all-reduce.7.cloned.1.call-done = bf16[128,256]{1,0:T(8,128)(2,1)} async-done(((bf16[128,256]{1,0:T(8,128)(2,1)}), bf16[128,256]{1,0:T(8,128)(2,1)}) %all-reduce.7.cloned.1.call-update) | async-done | bytes 65552 | tf_op jit(solution)/shard_map/while/body/eval_jaxpr/psum | solution.py:9
  125.9 0.9 select_select_fusion.2
  126.9 0.6 broadcast_select_fusion.2
  127.6 36.4 %all-reduce.7.cloned.1.call-done = bf16[128,256]{1,0:T(8,128)(2,1)} async-done(((bf16[128,256]{1,0:T(8,128)(2,1)}), bf16[128,256]{1,0:T(8,128)(2,1)}) %all-reduce.7.cloned.1.call-update) | async-done | bytes 65552 | tf_op jit(solution)/shard_map/while/body/eval_jaxpr/psum | solution.py:9
  164.0 0.9 select_select_fusion.2
  165.0 0.0 reduce-scatter.3.cloned.1.call-start
  165.0 0.3 fusion.9
  165.3 0.2 copy.18
  165.5 0.6 copy-done.5
  166.2 0.6 convolution_convert_fusion.1
  166.8 0.7 copy.15
  167.5 0.0 all-reduce.5.cloned.1.call-start
  167.6 0.1 convert_reduce_fusion
  167.7 0.6 copy-done.9
  168.4 0.7 copy-done.10
  169.0 0.6 dynamic-slice
  169.6 0.1 convolution_convert_fusion.2
  169.7 5.6 %all-reduce = bf16[4,128]{1,0:T(4,128)(2,1)S(1)} all-reduce(bf16[4,128]{1,0:T(4,128)(2,1)S(1)} %convolution_convert_fusion.2), channel_id=3, replica_groups=mesh['island'=2,'stripe'=4,'rep'=4] {'rep'}, use_global_device_ids=true, to_apply=%region_5.6.clone | all-reduce | flops 512 | bytes 2048
  175.4 0.7 fusion.22
  176.1 0.2 fusion.26
  176.2 11.9 %reduce-scatter.3.cloned.1.call-done = bf16[1,128,256]{2,1,0:T(8,128)(2,1)} async-done(((bf16[4,128,256]{2,1,0:T(8,128)(2,1)}), bf16[1,128,256]{2,1,0:T(8,128)(2,1)}) %reduce-scatter.3.cloned.1.call-update) | async-done | bytes 65552 | tf_op jit(solution)/shard_map/reduce_scatter | solution.py:39
  188.2 1.7 convert_reduce_fusion.1
  189.9 0.2 fusion.1
  190.1 0.9 convolution_bitcast_fusion
  191.0 5.8 %all_gather.3 = bf16[512,256]{1,0:T(8,128)(2,1)S(1)} all-gather(bf16[128,256]{1,0:T(8,128)(2,1)S(1)} %fusion.1), channel_id=1, replica_groups=mesh['island'=2,'stripe'=4,'rep'=4] {'rep'}, dimensions={0}, use_global_device_ids=true | all-gather | bytes 327680 | tf_op jit(solution)/shard_map/all_gather | solution.py:68
  196.8 0.3 fusion.4
  197.1 0.5 copy-done.8
  197.6 1.0 fusion.23
  198.6 0.0 reduce-scatter.5.cloned.1.call-start
  198.7 0.3 fusion.6
  198.9 0.2 copy.21
  199.2 0.6 convolution_convert_fusion
  199.8 0.7 copy.16
  200.5 33.5 %psum.37 = f32[256]{0:T(256)} all-reduce(f32[256]{0:T(256)S(1)} %get-tuple-element.151), channel_id=1, replica_groups=mesh['island'=2,'stripe'=4,'rep'=4] {'stripe','rep'}, use_global_device_ids=true, to_apply=%region_10.11 | all-reduce | flops 256 | bytes 2048 | tf_op jit(solution)/shard_map/psum | solution.py:63
  234.0 54.5 %all-reduce.5.cloned.1.call-done = (f32[256,256]{0,1:T(8,128)}, f32[256,256]{1,0:T(8,128)}) async-done(((f32[256,256]{0,1:T(8,128)}, f32[256,256]{1,0:T(8,128)}), (f32[256,256]{0,1:T(8,128)}, f32[256,256]{1,0:T(8,128)})) %all-reduce.5.cloned.1.call-update) | async-done | bytes 524304 | tf_op jit(solution)/shard_map/psum | solution.py:63
  288.5 1.8 copy.17
  290.3 21.4 %reduce-scatter.5.cloned.1.call-done = bf16[128,256]{1,0:T(8,128)(2,1)} async-done(((bf16[512,256]{1,0:T(8,128)(2,1)}), bf16[128,256]{1,0:T(8,128)(2,1)}) %reduce-scatter.5.cloned.1.call-update) | async-done | bytes 65552 | tf_op jit(solution)/shard_map/reduce_scatter | solution.py:77
  311.6 1.7 convolution_add_fusion
  313.3 0.7 copy.35
  (34 shorter events, 0.4 us)
Async XLA Ops:
  8.0 180.2 %copy-start = (bf16[256,256]{1,0:T(8,128)(2,1)S(1)}, bf16[256,256]{1,0:T(8,128)(2,1)}, u32[]{:S(2)}) copy-start(bf16[256,256]{1,0:T(8,128)(2,1)} %param.15) | copy-start | bytes 393220
  8.0 0.7 copy-start.6
  8.7 156.3 %copy-start.2 = (bf16[1,1,3,128,128]{4,3,2,1,0:T(8,128)(2,1)S(1)}, bf16[1,1,3,128,128]{4,3,2,1,0:T(8,128)(2,1)}, u32[]{:S(2)}) copy-start(bf16[1,1,3,128,128]{4,3,2,1,0:T(8,128)(2,1)} %param.11) | copy-start | bytes 294916
  8.7 40.4 %all-reduce.7.cloned.1.call-start = ((), (), s32[]{:S(2)}) async-start(), calls=%async_computation.5 | async-start | bytes 131072 | tf_op jit(solution)/shard_map/while/body/eval_jaxpr/psum | solution.py:9
  50.1 37.5 %all-reduce.7.cloned.1.call-start = ((), (), s32[]{:S(2)}) async-start(), calls=%async_computation.5 | async-start | bytes 131072 | tf_op jit(solution)/shard_map/while/body/eval_jaxpr/psum | solution.py:9
  88.5 37.4 %all-reduce.7.cloned.1.call-start = ((), (), s32[]{:S(2)}) async-start(), calls=%async_computation.5 | async-start | bytes 131072 | tf_op jit(solution)/shard_map/while/body/eval_jaxpr/psum | solution.py:9
  126.9 37.1 %all-reduce.7.cloned.1.call-start = ((), (), s32[]{:S(2)}) async-start(), calls=%async_computation.5 | async-start | bytes 131072 | tf_op jit(solution)/shard_map/while/body/eval_jaxpr/psum | solution.py:9
  165.0 23.2 %reduce-scatter.3.cloned.1.call-start = ((), (), s32[]{:S(2)}) async-start(), calls=%async_computation.2 | async-start | bytes 327680 | tf_op jit(solution)/shard_map/reduce_scatter | solution.py:39
  165.5 0.7 copy-start.5
  167.5 8.5 %copy-start.3 = (bf16[256,256]{1,0:T(8,128)(2,1)S(1)}, bf16[256,256]{1,0:T(8,128)(2,1)}, u32[]{:S(2)}) copy-start(bf16[256,256]{1,0:T(8,128)(2,1)} %param.14) | copy-start | bytes 393220
  167.5 8.5 %copy-start.1 = (bf16[128,256]{1,0:T(8,128)(2,1)S(1)}, bf16[128,256]{1,0:T(8,128)(2,1)}, u32[]{:S(2)}) copy-start(bf16[128,256]{1,0:T(8,128)(2,1)} %get-tuple-element.217) | copy-start | bytes 196612
  167.5 120.9 %all-reduce.5.cloned.1.call-start = ((), (), s32[]{:S(2)}) async-start(), calls=%async_computation.4 | async-start | bytes 1048576 | tf_op jit(solution)/shard_map/psum | solution.py:63
  167.7 0.7 copy-start.9
  168.4 0.7 copy-start.10
  176.1 12.1 %copy-start.7 = (bf16[128,256]{1,0:T(8,128)(2,1)S(1)}, bf16[128,256]{1,0:T(8,128)(2,1)}, u32[]{:S(2)}) copy-start(bf16[128,256]{1,0:T(8,128)(2,1)} %param.17) | copy-start | bytes 196612
  196.8 0.8 copy-start.8
  198.6 113.0 %reduce-scatter.5.cloned.1.call-start = ((), (), s32[]{:S(2)}) async-start(), calls=%async_computation.3 | async-start | bytes 327680 | tf_op jit(solution)/shard_map/reduce_scatter | solution.py:77
  290.2 23.1 %copy-start.4 = (f32[256,256]{1,0:T(8,128)S(1)}, f32[256,256]{1,0:T(8,128)}, u32[]{:S(2)}) copy-start(f32[256,256]{1,0:T(8,128)} %get-tuple-element.206) | copy-start | bytes 786436
Sparse Core Ops, SparseCore 0:
  12.4 36.6 all-reduce.6
  53.8 33.6 all-reduce.6
  92.2 33.6 all-reduce.6
  130.3 33.6 all-reduce.6
Sparse Core Ops, SparseCore 1:
  168.5 19.6 reduce-scatter.2
  198.7 89.7 all-reduce.4
  291.3 20.3 reduce-scatter.4
where the time goes:
time: 322 us; the launch traced here: 321 us
  waiting for transfers between devices  237 us (74%)
  blocking collectives  44.9 us (14%)
  between operations  15.6 us (5%)
  local copies, waits for them, and re-layouts  8.15 us (3%)
  other arithmetic  7.96 us (2%)
  matrix products  7.84 us (2%)
    psum x4, waiting for transfers between devices, broadcast(): return lax.psum(kept, axis)  149 us
    psum x1, waiting for transfers between devices, shards(): lax.psum((grad_self, grad_neigh, grad_bias), ('stripe', 'rep'))  54.5 us
    psum x1, blocking collectives, shards(): lax.psum((grad_self, grad_neigh, grad_bias), ('stripe', 'rep'))  33.5 us
    reduce_scatter x1, waiting for transfers between devices, shards(): lax.psum_scatter(term.reshape(edge * lax.axis_size('stripe'), width).asty...  21.4 us
    reduce_scatter x1, waiting for transfers between devices, shards(): lax.psum_scatter(partial_sum.astype(jnp.bfloat16), 'rep', scatter_dimensi...  11.9 us
  transfers between devices with their start and end apart: 7, of which 7 were waited for; matrix products, arithmetic and copies ran while one was open for 2% of the time, Pallas kernels for 0%

commit v1 on v0

v1 whole, which is shorter than its diff:
```python
import functools

import jax
import jax.numpy as jnp
from jax import lax
from jax.experimental import pallas as pl
from jax.experimental.pallas import tpu as pltpu
from jax.sharding import PartitionSpec as P

MESH = pl.DeviceIdType.MESH
BF16 = jnp.bfloat16
F32 = jnp.float32
PAD = 16


def matmul(a, b):
    return jnp.dot(a, b, preferred_element_type=F32)


def matmul_t(a, b):
    return lax.dot_general(a, b, (((1,), (1,)), ((), ())), preferred_element_type=F32)


def send(src, dst, sems, slot, device):
    return pltpu.make_async_remote_copy(
        src_ref=src,
        dst_ref=dst,
        send_sem=sems[0].at[slot],
        recv_sem=sems[1].at[slot],
        device_id=device,
        device_id_type=MESH,
    )


def kernel(
    stripes, reps, sub,
    row_ref, src_ref, feat_ref, tiles_ref, self_ref, neigh_ref, bias_ref, cot_ref,
    out_ref, gin_ref, gself_ref, gneigh_ref, gbias_ref,
    feat_buf, deg_send, deg_buf, agg_send, agg_buf, pull_buf, term_send, term_buf,
    rep_send, rep_buf, str_send, str_buf, all_str, all_rep, adj, adj_t,
    feat_s, feat_r, deg_s, deg_r, agg_s, agg_r, pull_s, pull_r, term_s, term_r,
    rep_s, rep_r, str_s, str_r, gst_s, gst_r, grp_s, grp_r,
):
    island = lax.axis_index("island")
    s = lax.axis_index("stripe")
    r = lax.axis_index("rep")
    edge, width = feat_ref.shape
    slots = tiles_ref.shape[2]

    def to_stripe(d):
        return (island, lax.rem(s + d, stripes), r)

    def to_rep(e):
        return (island, s, lax.rem(r + e, reps))

    barrier = pltpu.get_barrier_semaphore()
    for d in range(1, stripes):
        pl.semaphore_signal(barrier, inc=1, device_id=to_stripe(d), device_id_type=MESH)
    for e in range(1, reps):
        pl.semaphore_signal(barrier, inc=1, device_id=to_rep(e), device_id_type=MESH)
    pl.semaphore_wait(barrier, stripes + reps - 2)

    feat_copies = [
        send(feat_ref, feat_buf.at[d], (feat_s, feat_r), d, to_stripe(d)) for d in range(1, stripes)
    ]
    for copy in feat_copies:
        copy.start()

    tile = [tiles_ref[0, 0, k] for k in range(slots)]
    row = [row_ref[0, 0, k] for k in range(slots)]
    src = [src_ref[0, 0, k] for k in range(slots)]
    ones = jnp.ones((edge, edge), BF16)
    sums = [matmul(t, ones) for t in tile]
    for e in range(reps):
        q = lax.rem(r + e, reps)
        total = jnp.zeros((edge, edge), F32)
        for k in range(slots):
            total = total + jnp.where(row[k] == q, sums[k], 0.0)
        deg_send[e] = total.astype(BF16)
    deg_copies = [
        send(deg_send.at[e], deg_buf.at[e], (deg_s, deg_r), e, to_rep(e)) for e in range(1, reps)
    ]
    for copy in deg_copies:
        copy.start()

    zero = jnp.zeros((edge, edge), F32)
    tile_f = [t.astype(F32) for t in tile]
    tile_tf = [t.T for t in tile_f]

    def place(ref, e, d, values, q, t):
        total = zero
        for k in range(slots):
            total = total + jnp.where((row[k] == q) & (src[k] == t), values[k], 0.0)
        ref[e * edge:(e + 1) * edge, d * edge:(d + 1) * edge] = total.astype(BF16)

    for d in range(stripes):
        for e in range(reps):
            place(adj, e, d, tile_f, lax.rem(r + e, reps), lax.rem(s + stripes - d, stripes))
    for d in range(stripes):
        for e in range(reps):
            place(adj_t, d, e, tile_tf, lax.rem(r + reps - e, reps), lax.rem(s + d, stripes))

    feats = feat_ref[...]
    feats_t = feats.astype(F32).T.astype(BF16)
    pre_self = matmul(feats, self_ref[...]) + bias_ref[...].astype(F32)

    feat_buf[0] = feats
    for copy in feat_copies:
        copy.wait_recv()
    feat_all = feat_buf[...].reshape(stripes * edge, width)
    agg_copies = []
    for e in range(1, reps):
        agg_send[e] = matmul(adj[e * edge:(e + 1) * edge, :], feat_all).astype(BF16)
        copy = send(agg_send.at[e], agg_buf.at[e], (agg_s, agg_r), e, to_rep(e))
        copy.start()
        agg_copies.append(copy)
    agg = matmul(adj[0:edge, :], feat_all)
    degree = 1.0 + deg_send[0].astype(F32)
    for copy in deg_copies:
        copy.wait_recv()
    for e in range(1, reps):
        degree = degree + deg_buf[e].astype(F32)
    inverse = jnp.concatenate([1.0 / degree] * (width // edge), axis=1)
    for copy in agg_copies:
        copy.wait_recv()
    for e in range(1, reps):
        agg = agg + agg_buf[e].astype(F32)
    neigh = (agg * inverse).astype(BF16)

    pre = pre_self + matmul(neigh, neigh_ref[...])
    sigma = jax.nn.sigmoid(pre)
    slope = (cot_ref[...].astype(F32) * sigma * (1.0 + pre * (1.0 - sigma))).astype(BF16)

    pull_buf[0] = (matmul_t(slope, neigh_ref[...]) * inverse).astype(BF16)
    pull_copies = [
        send(pull_buf.at[0], pull_buf.at[e], (pull_s, pull_r), e, to_rep(e)) for e in range(1, reps)
    ]
    for copy in pull_copies:
        copy.start()

    chunk = rep_send.shape[1] - PAD
    neigh_t = neigh.astype(F32).T.astype(BF16)
    grad_bias = jnp.sum(slope.astype(F32), axis=0, keepdims=True)
    bias_rows = jnp.broadcast_to(grad_bias, (PAD, width)).astype(BF16)
    grads = jnp.concatenate([matmul(feats_t, slope), matmul(neigh_t, slope)], axis=0).astype(BF16)
    for c in range(reps):
        rep_send[c, :chunk] = grads[c * chunk:(c + 1) * chunk]
        rep_send[c, chunk:] = bias_rows
    rep_copies = [
        send(
            rep_send.at[lax.rem(r + e, reps)], rep_buf.at[e], (rep_s, rep_r), e, to_rep(e)
        )
        for e in range(1, reps)
    ]
    for copy in rep_copies:
        copy.start()
    out_ref[...] = (pre * sigma).astype(BF16)

    for copy in pull_copies:
        copy.wait_recv()
    pull_all = pull_buf[...].reshape(reps * edge, width)
    term_copies = []
    for d in range(1, stripes):
        term_send[d] = matmul(adj_t[d * edge:(d + 1) * edge, :], pull_all).astype(BF16)
        copy = send(term_send.at[d], term_buf.at[d], (term_s, term_r), d, to_stripe(d))
        copy.start()
        term_copies.append(copy)
    grad_input = matmul_t(slope, self_ref[...])
    grad_input = grad_input + matmul(adj_t[0:edge, :], pull_all).astype(BF16).astype(F32)

    share = rep_send[r].astype(F32)
    for copy in rep_copies:
        copy.wait_recv()
    for e in range(1, reps):
        share = share + rep_buf[e].astype(F32)
    if sub:
        share_b = share.astype(BF16)
        for c in range(stripes):
            str_send[c, :sub] = share_b[c * sub:(c + 1) * sub]
            str_send[c, sub:] = share_b[chunk:]
        str_copies = [
            send(
                str_send.at[lax.rem(s + d, stripes)], str_buf.at[d], (str_s, str_r), d, to_stripe(d)
            )
            for d in range(1, stripes)
        ]
        for copy in str_copies:
            copy.start()
        part = str_send[s].astype(F32)
        for copy in str_copies:
            copy.wait_recv()
        for d in range(1, stripes):
            part = part + str_buf[d].astype(F32)
        gbias_ref[...] = part[sub:sub + 1]
        all_str[s] = part[:sub].astype(BF16)
        gst_copies = [
            send(all_str.at[s], all_str.at[s], (gst_s, gst_r), d, to_stripe(d))
            for d in range(1, stripes)
        ]
        for copy in gst_copies:
            copy.start()
        for copy in gst_copies:
            copy.wait_recv()
        all_rep[r] = all_str[...].reshape(chunk, width)
    else:
        str_send[0] = share.astype(BF16)
        str_copies = [
            send(str_send.at[0], str_buf.at[d], (str_s, str_r), d, to_stripe(d))
            for d in range(1, stripes)
        ]
        for copy in str_copies:
            copy.start()
        part = share
        for copy in str_copies:
            copy.wait_recv()
        for d in range(1, stripes):
            part = part + str_buf[d].astype(F32)
        gbias_ref[...] = part[chunk:chunk + 1]
        all_rep[r] = part[:chunk].astype(BF16)
        gst_copies = []
    grp_copies = [
        send(all_rep.at[r], all_rep.at[r], (grp_s, grp_r), e, to_rep(e)) for e in range(1, reps)
    ]
    for copy in grp_copies:
        copy.start()

    for copy in term_copies:
        copy.wait_recv()
    for d in range(1, stripes):
        grad_input = grad_input + term_buf[d].astype(F32)
    gin_ref[...] = grad_input

    for copy in grp_copies:
        copy.wait_recv()
    half = reps // 2
    gself_ref[...] = all_rep[:half].reshape(half * chunk, width).astype(F32)
    gneigh_ref[...] = all_rep[half:].reshape(half * chunk, width).astype(F32)

    for copies in (
        feat_copies, deg_copies, agg_copies, pull_copies, rep_copies,
        term_copies, str_copies, gst_copies, grp_copies,
    ):
        for copy in copies:
            copy.wait_send()


def shards(features, tiles, tile_row, tile_src, self_weight, neigh_weight, bias, cotangent):
    stripes = lax.axis_size("stripe")
    reps = lax.axis_size("rep")
    edge, width = features.shape
    chunk = 2 * self_weight.shape[0] // reps
    sub = chunk // stripes if chunk % (PAD * stripes) == 0 else 0
    share = (stripes, sub + PAD, width) if sub else (stripes, chunk + PAD, width)
    vmem = pl.BlockSpec(memory_space=pltpu.VMEM)
    smem = pl.BlockSpec(memory_space=pltpu.SMEM)
    dma = pltpu.SemaphoreType.DMA
    by_rep = [dma((reps,)), dma((reps,))]
    by_stripe = [dma((stripes,)), dma((stripes,))]
    output, grad_input, grad_self, grad_neigh, grad_bias = pl.pallas_call(
        functools.partial(kernel, stripes, reps, sub),
        out_shape=(
            jax.ShapeDtypeStruct((edge, width), BF16),
            jax.ShapeDtypeStruct((edge, width), F32),
            jax.ShapeDtypeStruct(self_weight.shape, F32),
            jax.ShapeDtypeStruct(neigh_weight.shape, F32),
            jax.ShapeDtypeStruct((1, width), F32),
        ),
        in_specs=[smem, smem] + [vmem] * 6,
        out_specs=(vmem,) * 5,
        scratch_shapes=[
            pltpu.VMEM((stripes, edge, width), BF16),
            pltpu.VMEM((reps, edge, edge), BF16),
            pltpu.VMEM((reps, edge, edge), BF16),
            pltpu.VMEM((reps, edge, width), BF16),
            pltpu.VMEM((reps, edge, width), BF16),
            pltpu.VMEM((reps, edge, width), BF16),
            pltpu.VMEM((stripes, edge, width), BF16),
            pltpu.VMEM((stripes, edge, width), BF16),
            pltpu.VMEM((reps, chunk + PAD, width), BF16),
            pltpu.VMEM((reps, chunk + PAD, width), BF16),
            pltpu.VMEM(share, BF16),
            pltpu.VMEM(share, BF16),
            pltpu.VMEM((stripes, max(sub, PAD), width), BF16),
            pltpu.VMEM((reps, chunk, width), BF16),
            pltpu.VMEM((reps * edge, stripes * edge), BF16),
            pltpu.VMEM((stripes * edge, reps * edge), BF16),
        ]
        + by_stripe + by_rep + by_rep + by_rep + by_stripe
        + by_rep + by_stripe + by_stripe + by_rep,
        compiler_params=pltpu.CompilerParams(
            collective_id=0, has_side_effects=True, vmem_limit_bytes=48 * 2**20
        ),
    )(tile_row, tile_src, features, tiles, self_weight, neigh_weight, bias.reshape(1, width), cotangent)
    return output, grad_input, grad_self, grad_neigh, grad_bias.reshape(width)


def solution(mesh):
    return jax.shard_map(
        shards,
        mesh=mesh,
        in_specs=(
            P(("island", "stripe", "rep"), None),
            P(("island", "stripe"), "rep", None, None, None),
            P(("island", "stripe"), "rep", None),
            P(("island", "stripe"), "rep", None),
            P(),
            P(),
            P(),
            P(("island", "stripe", "rep"), None),
        ),
        out_specs=(
            P(("island", "stripe", "rep"), None),
            P(("island", "stripe", "rep"), None),
            P("island", None),
            P("island", None),
            P("island"),
        ),
        check_vma=False,
    )
```

time: 322 us -> 48.4 us (0.15)
  waiting for transfers between devices: 237 us -> 0 us
  blocking collectives: 44.9 us -> 0 us
  Pallas kernels: 0 us -> 39 us
  between operations: 15.6 us -> 0.67 us
  other arithmetic: 7.96 us -> 0 us
  matrix products: 7.84 us -> 0 us
    psum x5 -> x0, waiting for transfers between devices: 203 us -> none  [the longest x4 149 us: broadcast(): return lax.psum(kept, axis)]
    pallas_call x0 -> x1, Pallas kernels: none -> 39 us  [shards(): pl.pallas_call(functools.partial(kernel, stripes, reps, sub), out_shape=(...]
    psum x1 -> x0, blocking collectives: 33.5 us -> none  [shards(): lax.psum((grad_self, grad_neigh, grad_bias), ('stripe', 'rep'))]
    reduce_scatter x2 -> x0, waiting for transfers between devices: 33.3 us -> none  [the longest x1 21.4 us: shards(): lax.psum_scatter(term.reshape(edge * lax.axis_size('stripe'), width).asty...]
    dot_general x12 -> x0, matrix products: 7.84 us -> none  [the longest x1 1.74 us: shards(): jnp.dot(neigh, neigh_weight, preferred_element_type=jnp.float32)]
    select_n x8 -> x0, other arithmetic: 7.17 us -> none  [the longest x4 3.72 us: turn(): return jnp.where(match, block[None], slot_feats)]
    all_gather x1 -> x0, blocking collectives: 5.77 us -> none  [shards(): lax.all_gather(pull, 'rep', axis=0, tiled=True).reshape(reps, edge, width)]
    unnamed x1 -> x0, blocking collectives: 5.65 us -> none
  transfers between devices with their start and end apart: 7 -> 0, of which waited for: 7 -> 0; matrix products, arithmetic and copies ran while one was open for 2% -> 0% of each run, Pallas kernels for 0% -> 0%
where the time goes in v1:
time: 48.4 us; the launch traced here: 48 us
  Pallas kernels  39 us (81%)
  local copies, waits for them, and re-layouts  8.31 us (17%)
  between operations  0.67 us (1%)
    pallas_call x1, Pallas kernels, shards(): pl.pallas_call(functools.partial(kernel, stripes, reps, sub), out_shape=(...  39 us
    unnamed x19, local copies, waits for them, and re-layouts  7.64 us

profile of v1, /device:TPU:0, one launch (start us, length us, event | category | flops | bytes accessed | tf_op | source)
XLA Modules:
  0.0 48.0 jit_solution(6169693623327530037)
XLA Ops:
  0.6 0.0 copy-start.6
  0.6 0.0 copy-start.5
  0.7 0.7 %reshape.16.bias_ref = bf16[1,256]{1,0:T(2,128)(2,1)S(1)} reshape(bf16[256]{0:T(256)(128)(2,1)} %param.14) | data formatting | bytes 1024 | tf_op jit(solution)/shard_map/reshape | solution.py:293
  1.3 0.0 copy-done.6
  1.3 0.0 copy-done.5
  1.3 0.0 copy-start
  1.3 0.9 %copy-done = bf16[256,256]{1,0:T(8,128)(2,1)S(1)} copy-done((bf16[256,256]{1,0:T(8,128)(2,1)S(1)}, bf16[256,256]{1,0:T(8,128)(2,1)}, u32[]{:S(2)}) %copy-start) | copy-done | bytes 131096
  2.2 0.0 copy-start.1
  2.2 0.9 %copy-done.1 = bf16[256,256]{1,0:T(8,128)(2,1)S(1)} copy-done((bf16[256,256]{1,0:T(8,128)(2,1)S(1)}, bf16[256,256]{1,0:T(8,128)(2,1)}, u32[]{:S(2)}) %copy-start.1) | copy-done | bytes 131096
  3.1 0.0 copy-start.2
  3.1 0.9 %copy-done.2 = bf16[1,1,3,128,128]{4,3,2,1,0:T(8,128)(2,1)S(1)} copy-done((bf16[1,1,3,128,128]{4,3,2,1,0:T(8,128)(2,1)S(1)}, bf16[1,1,3,128,128]{4,3,2,1,0:T(8,128)(2,1)}, u32[]{:S(2)}) %copy-start.2) | copy-done | bytes 98328
  4.0 0.0 copy-start.3
  4.0 0.8 %copy-done.3 = bf16[128,256]{1,0:T(8,128)(2,1)S(1)} copy-done((bf16[128,256]{1,0:T(8,128)(2,1)S(1)}, bf16[128,256]{1,0:T(8,128)(2,1)}, u32[]{:S(2)}) %copy-start.3) | copy-done | bytes 65560
  4.9 0.0 copy-start.4
  4.9 0.8 %copy-done.4 = bf16[128,256]{1,0:T(8,128)(2,1)S(1)} copy-done((bf16[128,256]{1,0:T(8,128)(2,1)S(1)}, bf16[128,256]{1,0:T(8,128)(2,1)}, u32[]{:S(2)}) %copy-start.4) | copy-done | bytes 65560
  5.7 39.0 %shard_map.119 = (bf16[128,256]{1,0:T(8,128)(2,1)S(1)}, f32[128,256]{1,0:T(8,128)S(1)}, f32[256,256]{1,0:T(8,128)S(1)}, f32[256,256]{1,0:T(8,128)S(1)}, f32[1,256]{1,0:T(1,128)S(1)}) custom-call(s32[1,1,3]{2,1,0:T(1,128)S(1)} %copy-done.5, s32[1,1,3]{2,1,0:T(1,128)S(1)} %copy-done.6, bf16[128,256]{1,0:T(8,128)(2,1)S(1)} %copy-done.3, ...), custom_call_target="tpu_custom_call" | custom-call | tf_op jit(solution)/shard_map/pallas_call | solution.py:259
  44.7 0.6 %copy.18 = bf16[128,256]{1,0:T(8,128)(2,1)} copy(bf16[128,256]{1,0:T(8,128)(2,1)S(1)} %get-tuple-element.20) | data formatting | bytes 131072
  45.3 0.7 %copy.19 = f32[128,256]{1,0:T(8,128)} copy(f32[128,256]{1,0:T(8,128)S(1)} %get-tuple-element.21) | data formatting | bytes 262144
  46.0 0.7 %copy.20 = f32[256,256]{1,0:T(8,128)} copy(f32[256,256]{1,0:T(8,128)S(1)} %get-tuple-element.22) | data formatting | bytes 524288
  46.7 0.7 %copy.21 = f32[256,256]{1,0:T(8,128)} copy(f32[256,256]{1,0:T(8,128)S(1)} %get-tuple-element.23) | data formatting | bytes 524288
  47.4 0.6 %copy.22 = f32[256]{0:T(256)} copy(f32[256]{0:T(256)S(1)} %bitcast.1) | data formatting | bytes 2048
Async XLA Ops:
  0.6 0.7 %copy-start.6 = (s32[1,1,3]{2,1,0:T(1,128)S(1)}, s32[1,1,3]{2,1,0:T(1,128)}, u32[]{:S(2)}) copy-start(s32[1,1,3]{2,1,0:T(1,128)} %src_ref.1) | copy-start | bytes 40
  0.6 0.7 %copy-start.5 = (s32[1,1,3]{2,1,0:T(1,128)S(1)}, s32[1,1,3]{2,1,0:T(1,128)}, u32[]{:S(2)}) copy-start(s32[1,1,3]{2,1,0:T(1,128)} %row_ref.1) | copy-start | bytes 40
  1.3 0.9 %copy-start = (bf16[256,256]{1,0:T(8,128)(2,1)S(1)}, bf16[256,256]{1,0:T(8,128)(2,1)}, u32[]{:S(2)}) copy-start(bf16[256,256]{1,0:T(8,128)(2,1)} %self_ref.1) | copy-start | bytes 393220
  2.2 0.9 %copy-start.1 = (bf16[256,256]{1,0:T(8,128)(2,1)S(1)}, bf16[256,256]{1,0:T(8,128)(2,1)}, u32[]{:S(2)}) copy-start(bf16[256,256]{1,0:T(8,128)(2,1)} %neigh_ref.1) | copy-start | bytes 393220
  3.1 0.9 %copy-start.2 = (bf16[1,1,3,128,128]{4,3,2,1,0:T(8,128)(2,1)S(1)}, bf16[1,1,3,128,128]{4,3,2,1,0:T(8,128)(2,1)}, u32[]{:S(2)}) copy-start(bf16[1,1,3,128,128]{4,3,2,1,0:T(8,128)(2,1)} %tiles_ref.1) | copy-start | bytes 294916
  4.0 0.8 %copy-start.3 = (bf16[128,256]{1,0:T(8,128)(2,1)S(1)}, bf16[128,256]{1,0:T(8,128)(2,1)}, u32[]{:S(2)}) copy-start(bf16[128,256]{1,0:T(8,128)(2,1)} %feat_ref.1) | copy-start | bytes 196612
  4.9 0.8 %copy-start.4 = (bf16[128,256]{1,0:T(8,128)(2,1)S(1)}, bf16[128,256]{1,0:T(8,128)(2,1)}, u32[]{:S(2)}) copy-start(bf16[128,256]{1,0:T(8,128)(2,1)} %cot_ref.1) | copy-start | bytes 196612

commit v2 on v1

v2 whole, which is shorter than its diff:
```python
import functools

import jax
import jax.numpy as jnp
from jax import lax
from jax.experimental import pallas as pl
from jax.experimental.pallas import tpu as pltpu
from jax.sharding import PartitionSpec as P

MESH = pl.DeviceIdType.MESH
BF16 = jnp.bfloat16
F32 = jnp.float32
PAD = 16
HALVES = 2


def matmul(a, b):
    return jnp.dot(a, b, preferred_element_type=F32)


def matmul_t(a, b):
    return lax.dot_general(a, b, (((1,), (1,)), ((), ())), preferred_element_type=F32)


def send(src, dst, sems, slot, device):
    return pltpu.make_async_remote_copy(
        src_ref=src,
        dst_ref=dst,
        send_sem=sems[0].at[slot],
        recv_sem=sems[1].at[slot],
        device_id=device,
        device_id_type=MESH,
    )


def kernel(
    stripes, reps, sub,
    row_hbm, src_hbm, feat_hbm, tiles_hbm, self_hbm, neigh_hbm, bias_hbm, cot_hbm,
    out_hbm, gin_hbm, all_hbm, gbias_hbm,
    row_ref, src_ref, feat_ref, tiles_ref, self_ref, neigh_ref, bias_ref, cot_ref, load_sem,
    out_ref, gin_ref, all_rep, gbias_ref, store_sem,
    feat_buf, deg_send, deg_buf, agg_send, agg_buf, pull_buf, term_send, term_buf,
    rep_send, rep_buf, str_send, str_buf, adj, adj_t,
    feat_s, feat_r, deg_s, deg_r, agg_s, agg_r, pull_s, pull_r, term_s, term_r,
    rep_s, rep_r, str_s, str_r, gst_s, gst_r, grp_s, grp_r,
):
    island = lax.axis_index("island")
    s = lax.axis_index("stripe")
    r = lax.axis_index("rep")
    edge, width = feat_ref.shape
    slots = tiles_ref.shape[2]
    half = width // HALVES
    cols = [slice(h * half, (h + 1) * half) for h in range(HALVES)]

    def to_stripe(d):
        return (island, lax.rem(s + d, stripes), r)

    def to_rep(e):
        return (island, s, lax.rem(r + e, reps))

    load_feat, load_tiles, load_row, load_src, load_self, load_neigh, load_bias, load_cot = loads = [
        pltpu.make_async_copy(hbm, ref, load_sem.at[i])
        for i, (hbm, ref) in enumerate(
            (
                (feat_hbm, feat_ref),
                (tiles_hbm, tiles_ref),
                (row_hbm, row_ref),
                (src_hbm, src_ref),
                (self_hbm, self_ref),
                (neigh_hbm, neigh_ref),
                (bias_hbm, bias_ref),
                (cot_hbm, cot_ref),
            )
        )
    ]
    store_out, store_gin, store_all, store_gbias = stores = [
        pltpu.make_async_copy(ref, hbm, store_sem.at[i])
        for i, (ref, hbm) in enumerate(
            ((out_ref, out_hbm), (gin_ref, gin_hbm), (all_rep, all_hbm), (gbias_ref, gbias_hbm))
        )
    ]
    pending = []

    barrier = pltpu.get_barrier_semaphore()
    for d in range(1, stripes):
        pl.semaphore_signal(barrier, inc=1, device_id=to_stripe(d), device_id_type=MESH)
    for e in range(1, reps):
        pl.semaphore_signal(barrier, inc=1, device_id=to_rep(e), device_id_type=MESH)
    for load in loads:
        load.start()
    load_feat.wait()
    pl.semaphore_wait(barrier, stripes + reps - 2)

    feat_copies = [
        [
            send(
                feat_ref.at[:, c], feat_buf.at[d, :, c], (feat_s, feat_r), (d, h), to_stripe(d)
            )
            for d in range(1, stripes)
        ]
        for h, c in enumerate(cols)
    ]
    for copies in feat_copies:
        for copy in copies:
            copy.start()
        pending += copies

    for load in (load_tiles, load_row, load_src):
        load.wait()
    tile = [tiles_ref[0, 0, k] for k in range(slots)]
    row = [row_ref[0, 0, k] for k in range(slots)]
    src = [src_ref[0, 0, k] for k in range(slots)]
    ones = jnp.ones((edge, edge), BF16)
    sums = [matmul(t, ones) for t in tile]
    for e in range(reps):
        q = lax.rem(r + e, reps)
        total = jnp.zeros((edge, edge), F32)
        for k in range(slots):
            total = total + jnp.where(row[k] == q, sums[k], 0.0)
        deg_send[e] = total.astype(BF16)
    deg_copies = [
        send(deg_send.at[e], deg_buf.at[e], (deg_s, deg_r), e, to_rep(e)) for e in range(1, reps)
    ]
    for copy in deg_copies:
        copy.start()
    pending += deg_copies

    zero = jnp.zeros((edge, edge), F32)
    tile_f = [t.astype(F32) for t in tile]
    tile_tf = [t.T for t in tile_f]

    def place(ref, e, d, values, q, t):
        total = zero
        for k in range(slots):
            total = total + jnp.where((row[k] == q) & (src[k] == t), values[k], 0.0)
        ref[e * edge:(e + 1) * edge, d * edge:(d + 1) * edge] = total.astype(BF16)

    for d in range(stripes):
        for e in range(reps):
            place(adj, e, d, tile_f, lax.rem(r + e, reps), lax.rem(s + stripes - d, stripes))
    for d in range(stripes):
        for e in range(reps):
            place(adj_t, d, e, tile_tf, lax.rem(r + reps - e, reps), lax.rem(s + d, stripes))

    load_self.wait()
    load_bias.wait()
    load_neigh.wait()
    load_cot.wait()
    feats = feat_ref[...]
    feats_t = feats.astype(F32).T.astype(BF16)
    feat_buf[0] = feats
    pre = matmul(feats, self_ref[...]) + bias_ref[...].reshape(1, width).astype(F32)
    degree = 1.0 + deg_send[0].astype(F32)
    for copy in deg_copies:
        copy.wait_recv()
    for e in range(1, reps):
        degree = degree + deg_buf[e].astype(F32)
    inverse = jnp.concatenate([1.0 / degree] * (width // edge), axis=1)

    agg_copies = []
    agg = []
    for h, c in enumerate(cols):
        for copy in feat_copies[h]:
            copy.wait_recv()
        feat_all = feat_buf[:, :, c].reshape(stripes * edge, half)
        partial = matmul(adj[...], feat_all)
        agg_copies.append([])
        for e in range(1, reps):
            agg_send[e, :, c] = partial[e * edge:(e + 1) * edge].astype(BF16)
            copy = send(
                agg_send.at[e, :, c], agg_buf.at[e, :, c], (agg_s, agg_r), (e, h), to_rep(e)
            )
            copy.start()
            agg_copies[h].append(copy)
        pending += agg_copies[h]
        agg.append(partial[:edge])
    neigh = []
    for h, c in enumerate(cols):
        for copy in agg_copies[h]:
            copy.wait_recv()
        for e in range(1, reps):
            agg[h] = agg[h] + agg_buf[e, :, c].astype(F32)
        neigh.append((agg[h] * inverse[:, c]).astype(BF16))
        pre = pre + matmul(neigh[h], neigh_ref[c, :])
    sigma = jax.nn.sigmoid(pre)
    slope = (cot_ref[...].astype(F32) * sigma * (1.0 + pre * (1.0 - sigma))).astype(BF16)

    chunk = rep_send.shape[1] - PAD
    grad_bias = jnp.sum(slope.astype(F32), axis=0, keepdims=True)
    bias_rows = jnp.broadcast_to(grad_bias, (PAD, width)).astype(BF16)
    lhs = [feats_t] + [n.astype(F32).T.astype(BF16) for n in neigh]
    grads = jnp.concatenate([matmul(a, slope) for a in lhs], axis=0).astype(BF16)
    for c in range(reps):
        rep_send[c, :chunk] = grads[c * chunk:(c + 1) * chunk]
        rep_send[c, chunk:] = bias_rows
    rep_copies = [
        send(
            rep_send.at[lax.rem(r + e, reps)], rep_buf.at[e], (rep_s, rep_r), e, to_rep(e)
        )
        for e in range(1, reps)
    ]
    for copy in rep_copies:
        copy.start()
    pending += rep_copies

    pull_copies = []
    for h, c in enumerate(cols):
        pull_buf[0, :, c] = (matmul_t(slope, neigh_ref[c, :]) * inverse[:, c]).astype(BF16)
        pull_copies.append(
            [
                send(
                    pull_buf.at[0, :, c], pull_buf.at[e, :, c], (pull_s, pull_r), (e, h), to_rep(e)
                )
                for e in range(1, reps)
            ]
        )
        for copy in pull_copies[h]:
            copy.start()
        pending += pull_copies[h]
    out_ref[...] = (pre * sigma).astype(BF16)
    store_out.start()
    grad_input = matmul_t(slope, self_ref[...])

    term_copies = []
    own_term = []

    def terms(h, c):
        for copy in pull_copies[h]:
            copy.wait_recv()
        pull_all = pull_buf[:, :, c].reshape(reps * edge, half)
        term = matmul(adj_t[...], pull_all).astype(BF16)
        for d in range(1, stripes):
            term_send[d, :, c] = term[d * edge:(d + 1) * edge]
            copy = send(
                term_send.at[d, :, c], term_buf.at[d, :, c], (term_s, term_r), (d, h), to_stripe(d)
            )
            copy.start()
            term_copies.append(copy)
            pending.append(copy)
        own_term.append(term[:edge].astype(F32))

    share = rep_send[r].astype(F32)
    for copy in rep_copies:
        copy.wait_recv()
    for e in range(1, reps):
        share = share + rep_buf[e].astype(F32)
    share = share.astype(BF16)
    if sub:
        for c in range(stripes):
            str_send[c, :sub] = share[c * sub:(c + 1) * sub]
            str_send[c, sub:] = share[chunk:]
        str_copies = [
            send(
                str_send.at[lax.rem(s + d, stripes)], str_buf.at[d], (str_s, str_r), d, to_stripe(d)
            )
            for d in range(1, stripes)
        ]
        part = str_send[s].astype(F32)
    else:
        str_send[0] = share
        str_copies = [
            send(str_send.at[0], str_buf.at[d], (str_s, str_r), d, to_stripe(d))
            for d in range(1, stripes)
        ]
        part = share.astype(F32)
    for copy in str_copies:
        copy.start()
    pending += str_copies
    for h in range(HALVES - 1):
        terms(h, cols[h])
    for copy in str_copies:
        copy.wait_recv()
    for d in range(1, stripes):
        part = part + str_buf[d].astype(F32)
    rows = sub if sub else chunk
    gbias_ref[...] = part[rows]
    store_gbias.start()
    grp_copies = []

    def forward(t):
        for e in range(1, reps):
            share_rows = all_rep.at[r, pl.ds(t * rows, rows)]
            copy = send(
                share_rows, share_rows, (grp_s, grp_r), (e, t if sub else 0), to_rep(e)
            )
            copy.start()
            grp_copies.append(copy)
            pending.append(copy)

    if sub:
        all_rep[r, pl.ds(pl.multiple_of(s * rows, rows), rows)] = part[:rows].astype(BF16)
        gst_copies = [
            send(
                all_rep.at[r, pl.ds(pl.multiple_of(s * rows, rows), rows)],
                all_rep.at[r, pl.ds(pl.multiple_of(s * rows, rows), rows)],
                (gst_s, gst_r), d, to_stripe(d),
            )
            for d in range(1, stripes)
        ]
        for copy in gst_copies:
            copy.start()
        pending += gst_copies
        forward(s)
        terms(HALVES - 1, cols[HALVES - 1])
        for d, copy in enumerate(gst_copies, 1):
            copy.wait_recv()
            forward(lax.rem(s + stripes - d, stripes))
    else:
        all_rep[r] = part[:rows].astype(BF16)
        forward(0)
        terms(HALVES - 1, cols[HALVES - 1])

    grad_input = grad_input + jnp.concatenate(own_term, axis=1)
    for copy in term_copies:
        copy.wait_recv()
    for d in range(1, stripes):
        grad_input = grad_input + term_buf[d].astype(F32)
    gin_ref[...] = grad_input
    store_gin.start()

    for copy in grp_copies:
        copy.wait_recv()
    store_all.start()
    for copy in pending:
        copy.wait_send()
    for store in stores:
        store.wait()


def finish(
    out_in, gin_in, all_in, gbias_in, out_hbm, gin_hbm, gself_hbm, gneigh_hbm, gbias_hbm,
    out_ref, gin_ref, all_ref, gbias_ref, gself_ref, gneigh_ref, load_sem, store_sem,
):
    loads = [
        pltpu.make_async_copy(hbm, ref, load_sem.at[i])
        for i, (hbm, ref) in enumerate(
            ((all_in, all_ref), (gin_in, gin_ref), (out_in, out_ref), (gbias_in, gbias_ref))
        )
    ]
    stores = [
        pltpu.make_async_copy(ref, hbm, store_sem.at[i])
        for i, (ref, hbm) in enumerate(
            (
                (gself_ref, gself_hbm),
                (gneigh_ref, gneigh_hbm),
                (gin_ref, gin_hbm),
                (out_ref, out_hbm),
                (gbias_ref, gbias_hbm),
            )
        )
    ]
    for load in loads:
        load.start()
    for load in loads:
        load.wait()
    for store in stores[2:]:
        store.start()
    middle = all_ref.shape[0] // 2
    gself_ref[...] = all_ref[:middle].reshape(gself_ref.shape).astype(F32)
    stores[0].start()
    gneigh_ref[...] = all_ref[middle:].reshape(gneigh_ref.shape).astype(F32)
    stores[1].start()
    for store in stores:
        store.wait()


def shards(features, tiles, tile_row, tile_src, self_weight, neigh_weight, bias, cotangent):
    stripes = lax.axis_size("stripe")
    reps = lax.axis_size("rep")
    edge, width = features.shape
    chunk = 2 * self_weight.shape[0] // reps
    sub = chunk // stripes if chunk % (PAD * stripes) == 0 else 0
    share = (stripes, sub + PAD, width) if sub else (stripes, chunk + PAD, width)
    hbm = pl.BlockSpec(memory_space=pl.ANY)
    dma = pltpu.SemaphoreType.DMA
    by_rep = [dma((reps,)), dma((reps,))]
    by_stripe = [dma((stripes,)), dma((stripes,))]
    by_rep_half = [dma((reps, HALVES)), dma((reps, HALVES))]
    by_stripe_half = [dma((stripes, HALVES)), dma((stripes, HALVES))]
    by_rep_stripe = [dma((reps, stripes)), dma((reps, stripes))]
    out_shape = (
        jax.ShapeDtypeStruct((edge, width), BF16),
        jax.ShapeDtypeStruct((edge, width), F32),
        jax.ShapeDtypeStruct(self_weight.shape, F32),
        jax.ShapeDtypeStruct(neigh_weight.shape, F32),
        jax.ShapeDtypeStruct((width,), F32),
    )
    shares = jax.ShapeDtypeStruct((reps, chunk, width), BF16)
    staged = (out_shape[0], out_shape[1], shares, out_shape[4])
    results = pl.pallas_call(
        functools.partial(kernel, stripes, reps, sub),
        out_shape=staged,
        in_specs=[hbm] * 8,
        out_specs=(hbm,) * 4,
        scratch_shapes=[
            pltpu.SMEM(tile_row.shape, jnp.int32),
            pltpu.SMEM(tile_src.shape, jnp.int32),
            pltpu.VMEM(features.shape, BF16),
            pltpu.VMEM(tiles.shape, BF16),
            pltpu.VMEM(self_weight.shape, BF16),
            pltpu.VMEM(neigh_weight.shape, BF16),
            pltpu.VMEM(bias.shape, BF16),
            pltpu.VMEM(cotangent.shape, BF16),
            dma((8,)),
            *(pltpu.VMEM(out.shape, out.dtype) for out in staged),
            dma((4,)),
            pltpu.VMEM((stripes, edge, width), BF16),
            pltpu.VMEM((reps, edge, edge), BF16),
            pltpu.VMEM((reps, edge, edge), BF16),
            pltpu.VMEM((reps, edge, width), BF16),
            pltpu.VMEM((reps, edge, width), BF16),
            pltpu.VMEM((reps, edge, width), BF16),
            pltpu.VMEM((stripes, edge, width), BF16),
            pltpu.VMEM((stripes, edge, width), BF16),
            pltpu.VMEM((reps, chunk + PAD, width), BF16),
            pltpu.VMEM((reps, chunk + PAD, width), BF16),
            pltpu.VMEM(share, BF16),
            pltpu.VMEM(share, BF16),
            pltpu.VMEM((reps * edge, stripes * edge), BF16),
            pltpu.VMEM((stripes * edge, reps * edge), BF16),
        ]
        + by_stripe_half + by_rep + by_rep_half + by_rep_half + by_stripe_half
        + by_rep + by_stripe + by_stripe + by_rep_stripe,
        compiler_params=pltpu.CompilerParams(
            collective_id=0, has_side_effects=True, vmem_limit_bytes=60 * 2**20
        ),
    )(tile_row, tile_src, features, tiles, self_weight, neigh_weight, bias, cotangent)
    return pl.pallas_call(
        finish,
        out_shape=out_shape,
        in_specs=[hbm] * 4,
        out_specs=(hbm,) * 5,
        scratch_shapes=[
            *(pltpu.VMEM(out.shape, out.dtype) for out in staged + out_shape[2:4]),
            dma((4,)),
            dma((5,)),
        ],
        compiler_params=pltpu.CompilerParams(vmem_limit_bytes=60 * 2**20),
    )(*results)


def solution(mesh):
    return jax.shard_map(
        shards,
        mesh=mesh,
        in_specs=(
            P(("island", "stripe", "rep"), None),
            P(("island", "stripe"), "rep", None, None, None),
            P(("island", "stripe"), "rep", None),
            P(("island", "stripe"), "rep", None),
            P(),
            P(),
            P(),
            P(("island", "stripe", "rep"), None),
        ),
        out_specs=(
            P(("island", "stripe", "rep"), None),
            P(("island", "stripe", "rep"), None),
            P("island", None),
            P("island", None),
            P("island"),
        ),
        check_vma=False,
    )
```

time: 48.4 us -> 37.5 us (0.77)
  local copies, waits for them, and re-layouts: 8.31 us -> 0 us
  Pallas kernels: 39 us -> 36.7 us
    unnamed x19 -> x0, local copies, waits for them, and re-layouts: 7.64 us -> none
    pallas_call x1 -> x2, Pallas kernels: 39 us -> 36.7 us  [the longest x1 34.7 us: shards(): pl.pallas_call(functools.partial(kernel, stripes, reps, sub), out_shape=s...]
    reshape x1 -> x0, local copies, waits for them, and re-layouts: 0.67 us -> none  [shards(): bias.reshape(1, width)]
where the time goes in v2:
time: 37.5 us; the launch traced here: 37.3 us
  Pallas kernels  36.7 us (98%)
  between operations  0.64 us (2%)
    pallas_call x1, Pallas kernels, shards(): pl.pallas_call(functools.partial(kernel, stripes, reps, sub), out_shape=s...  34.7 us
    pallas_call x1, Pallas kernels, shards(): pl.pallas_call(finish, out_shape=out_shape, in_specs=[hbm] * 4, out_specs...  1.93 us

profile of v2, /device:TPU:0, one launch (start us, length us, event | category | flops | bytes accessed | tf_op | source)
XLA Modules:
  0.0 37.3 jit_solution(1522558357020046061)
XLA Ops:
  0.6 34.7 %shard_map.119 = (bf16[128,256]{1,0:T(8,128)(2,1)}, f32[128,256]{1,0:T(8,128)}, bf16[4,128,256]{2,1,0:T(8,128)(2,1)}, f32[256]{0:T(256)}) custom-call(s32[1,1,3]{2,1,0:T(1,128)} %row_hbm.1, s32[1,1,3]{2,1,0:T(1,128)} %src_hbm.1, bf16[128,256]{1,0:T(8,128)(2,1)} %feat_hbm.1, bf16[1,1,3,128,128]{4,3,2,1,0:T(8,128)(2,1)} %tiles_hbm.1, ...), custom_call_target="tpu_custom_call" | custom-call | tf_op jit(solution)/shard_map/pallas_call | solution.py:390
  35.4 1.9 %shard_map.120 = (bf16[128,256]{1,0:T(8,128)(2,1)}, f32[128,256]{1,0:T(8,128)}, f32[256,256]{1,0:T(8,128)}, f32[256,256]{1,0:T(8,128)}, f32[256]{0:T(256)}) custom-call(bf16[128,256]{1,0:T(8,128)(2,1)} %get-tuple-element.9.out_in, f32[128,256]{1,0:T(8,128)} %get-tuple-element.10.gin_in, bf16[4,128,256]{2,1,0:T(8,128)(2,1)} %get-tuple-element.11.all_in, ...), custom_call_target="tpu_custom_call" | custom-call | tf_op jit(solution)/shard_map/pallas_call | solution.py:428

commit v3 on v2

--- a/solution.py
+++ b/solution.py
@@ -12,6 +12,7 @@
 F32 = jnp.float32
 PAD = 16
 HALVES = 2
+CORES = 2
 
 
 def matmul(a, b):
@@ -34,15 +35,15 @@
 
 
 def kernel(
-    stripes, reps, sub,
+    stripes, reps, owners,
     row_hbm, src_hbm, feat_hbm, tiles_hbm, self_hbm, neigh_hbm, bias_hbm, cot_hbm,
     out_hbm, gin_hbm, all_hbm, gbias_hbm,
     row_ref, src_ref, feat_ref, tiles_ref, self_ref, neigh_ref, bias_ref, cot_ref, load_sem,
     out_ref, gin_ref, all_rep, gbias_ref, store_sem,
     feat_buf, deg_send, deg_buf, agg_send, agg_buf, pull_buf, term_send, term_buf,
-    rep_send, rep_buf, str_send, str_buf, adj, adj_t,
+    grads, core_buf, chip_send, chip_buf, adj, adj_t,
     feat_s, feat_r, deg_s, deg_r, agg_s, agg_r, pull_s, pull_r, term_s, term_r,
-    rep_s, rep_r, str_s, str_r, gst_s, gst_r, grp_s, grp_r,
+    core_s, core_r, chip_s, chip_r, all_s, all_r, pair_s, pair_r,
 ):
     island = lax.axis_index("island")
     s = lax.axis_index("stripe")
@@ -81,15 +82,31 @@
     ]
     pending = []
 
+    core = lax.rem(r, CORES)
+    chips = reps // CORES
+    others = [(d, x) for d in range(stripes) for x in range(chips)][1:]
+
+    def chip_at(d, x):
+        return lax.rem(s + d, stripes), lax.rem(r // CORES + x, chips)
+
+    def to_chip(d, x):
+        stripe, chip = chip_at(d, x)
+        return (island, stripe, chip * CORES + core)
+
+    def number(d, x):
+        stripe, chip = chip_at(d, x)
+        return stripe * chips + chip
+
+    partner = (island, s, r + 1 - 2 * core)
+
     barrier = pltpu.get_barrier_semaphore()
-    for d in range(1, stripes):
-        pl.semaphore_signal(barrier, inc=1, device_id=to_stripe(d), device_id_type=MESH)
-    for e in range(1, reps):
-        pl.semaphore_signal(barrier, inc=1, device_id=to_rep(e), device_id_type=MESH)
+    greeted = [to_chip(d, x) for d, x in others] + [to_rep(e) for e in range(1, reps, 2)]
+    for device in greeted:
+        pl.semaphore_signal(barrier, inc=1, device_id=device, device_id_type=MESH)
     for load in loads:
         load.start()
     load_feat.wait()
-    pl.semaphore_wait(barrier, stripes + reps - 2)
+    pl.semaphore_wait(barrier, len(greeted))
 
     feat_copies = [
         [
@@ -185,27 +202,18 @@
     sigma = jax.nn.sigmoid(pre)
     slope = (cot_ref[...].astype(F32) * sigma * (1.0 + pre * (1.0 - sigma))).astype(BF16)
 
-    chunk = rep_send.shape[1] - PAD
+    grads[0] = matmul(feats_t, slope).astype(BF16)
+    neigh_t = jnp.concatenate([n.astype(F32).T.astype(BF16) for n in neigh], axis=0)
+    grads[1] = matmul(neigh_t, slope).astype(BF16)
+    core_copy = send(grads.at[1 - core], core_buf, (core_s, core_r), 0, partner)
+    core_copy.start()
+    pending.append(core_copy)
     grad_bias = jnp.sum(slope.astype(F32), axis=0, keepdims=True)
-    bias_rows = jnp.broadcast_to(grad_bias, (PAD, width)).astype(BF16)
-    lhs = [feats_t] + [n.astype(F32).T.astype(BF16) for n in neigh]
-    grads = jnp.concatenate([matmul(a, slope) for a in lhs], axis=0).astype(BF16)
-    for c in range(reps):
-        rep_send[c, :chunk] = grads[c * chunk:(c + 1) * chunk]
-        rep_send[c, chunk:] = bias_rows
-    rep_copies = [
-        send(
-            rep_send.at[lax.rem(r + e, reps)], rep_buf.at[e], (rep_s, rep_r), e, to_rep(e)
-        )
-        for e in range(1, reps)
-    ]
-    for copy in rep_copies:
-        copy.start()
-    pending += rep_copies
+    pull_buf[0, edge:] = jnp.broadcast_to(grad_bias, (PAD, width)).astype(BF16)
 
     pull_copies = []
     for h, c in enumerate(cols):
-        pull_buf[0, :, c] = (matmul_t(slope, neigh_ref[c, :]) * inverse[:, c]).astype(BF16)
+        pull_buf[0, :edge, c] = (matmul_t(slope, neigh_ref[c, :]) * inverse[:, c]).astype(BF16)
         pull_copies.append(
             [
                 send(
@@ -217,20 +225,52 @@
         for copy in pull_copies[h]:
             copy.start()
         pending += pull_copies[h]
+
+    rows = grads.shape[1] // owners
+    me = number(0, 0)
+
+    def when(index, step):
+        if owners == stripes * chips:
+            step()
+        else:
+            pl.when(index < owners)(step)
+
+    def share_of(ref, index):
+        return ref.at[pl.ds(pl.multiple_of(index * rows, rows), rows)]
+
+    core_copy.wait_recv()
+    chip_send[...] = (grads[core].astype(F32) + core_buf[...].astype(F32)).astype(BF16)
+    chip_copies = [
+        send(
+            share_of(chip_send, lax.rem(number(d, x), owners)), chip_buf.at[n],
+            (chip_s, chip_r), n, to_chip(d, x),
+        )
+        for n, (d, x) in enumerate(others)
+    ]
+    for (d, x), copy in zip(others, chip_copies):
+        when(number(d, x), copy.start)
+
     out_ref[...] = (pre * sigma).astype(BF16)
     store_out.start()
     grad_input = matmul_t(slope, self_ref[...])
 
     term_copies = []
     own_term = []
+    own_bias = []
 
     def terms(h, c):
         for copy in pull_copies[h]:
             copy.wait_recv()
-        pull_all = pull_buf[:, :, c].reshape(reps * edge, half)
+        pull_all = pull_buf[:, :edge, c].reshape(reps * edge, half)
+        bias_sum = grad_bias[:, c]
+        for e in range(1, reps):
+            bias_sum = bias_sum + pull_buf[e, edge:, c].astype(F32)[:1]
+        own_bias.append(bias_sum)
+        bias_rows = jnp.broadcast_to(bias_sum, (PAD, half)).astype(BF16)
         term = matmul(adj_t[...], pull_all).astype(BF16)
         for d in range(1, stripes):
-            term_send[d, :, c] = term[d * edge:(d + 1) * edge]
+            term_send[d, edge:, c] = bias_rows
+            term_send[d, :edge, c] = term[d * edge:(d + 1) * edge]
             copy = send(
                 term_send.at[d, :, c], term_buf.at[d, :, c], (term_s, term_r), (d, h), to_stripe(d)
             )
@@ -239,88 +279,60 @@
             pending.append(copy)
         own_term.append(term[:edge].astype(F32))
 
-    share = rep_send[r].astype(F32)
-    for copy in rep_copies:
-        copy.wait_recv()
-    for e in range(1, reps):
-        share = share + rep_buf[e].astype(F32)
-    share = share.astype(BF16)
-    if sub:
-        for c in range(stripes):
-            str_send[c, :sub] = share[c * sub:(c + 1) * sub]
-            str_send[c, sub:] = share[chunk:]
-        str_copies = [
-            send(
-                str_send.at[lax.rem(s + d, stripes)], str_buf.at[d], (str_s, str_r), d, to_stripe(d)
-            )
-            for d in range(1, stripes)
-        ]
-        part = str_send[s].astype(F32)
-    else:
-        str_send[0] = share
-        str_copies = [
-            send(str_send.at[0], str_buf.at[d], (str_s, str_r), d, to_stripe(d))
-            for d in range(1, stripes)
-        ]
-        part = share.astype(F32)
-    for copy in str_copies:
-        copy.start()
-    pending += str_copies
     for h in range(HALVES - 1):
         terms(h, cols[h])
-    for copy in str_copies:
-        copy.wait_recv()
-    for d in range(1, stripes):
-        part = part + str_buf[d].astype(F32)
-    rows = sub if sub else chunk
-    gbias_ref[...] = part[rows]
-    store_gbias.start()
-    grp_copies = []
-
-    def forward(t):
-        for e in range(1, reps):
-            share_rows = all_rep.at[r, pl.ds(t * rows, rows)]
-            copy = send(
-                share_rows, share_rows, (grp_s, grp_r), (e, t if sub else 0), to_rep(e)
-            )
+
+    def total():
+        part = share_of(chip_send, me)[...].astype(F32)
+        for n, copy in enumerate(chip_copies):
+            copy.wait_recv()
+            part = part + chip_buf[n].astype(F32)
+        mine = share_of(all_rep.at[core], me)
+        mine[...] = part.astype(BF16)
+        for copy in all_copies:
             copy.start()
-            grp_copies.append(copy)
-            pending.append(copy)
-
-    if sub:
-        all_rep[r, pl.ds(pl.multiple_of(s * rows, rows), rows)] = part[:rows].astype(BF16)
-        gst_copies = [
-            send(
-                all_rep.at[r, pl.ds(pl.multiple_of(s * rows, rows), rows)],
-                all_rep.at[r, pl.ds(pl.multiple_of(s * rows, rows), rows)],
-                (gst_s, gst_r), d, to_stripe(d),
-            )
-            for d in range(1, stripes)
-        ]
-        for copy in gst_copies:
-            copy.start()
-        pending += gst_copies
-        forward(s)
-        terms(HALVES - 1, cols[HALVES - 1])
-        for d, copy in enumerate(gst_copies, 1):
-            copy.wait_recv()
-            forward(lax.rem(s + stripes - d, stripes))
-    else:
-        all_rep[r] = part[:rows].astype(BF16)
-        forward(0)
-        terms(HALVES - 1, cols[HALVES - 1])
+
+    def spread_share(index, n):
+        rows_ref = share_of(all_rep.at[core], lax.rem(index, owners))
+        return send(rows_ref, rows_ref, (pair_s, pair_r), n, partner)
+
+    mine = share_of(all_rep.at[core], lax.rem(me, owners))
+    all_copies = [
+        send(mine, mine, (all_s, all_r), n, to_chip(d, x)) for n, (d, x) in enumerate(others)
+    ]
+    when(me, total)
+    pair_copies = [(me, spread_share(me, len(others)))]
+    when(me, pair_copies[0][1].start)
+    terms(HALVES - 1, cols[HALVES - 1])
+    for n, (d, x) in enumerate(others):
+        index = number(stripes - d, chips - x)
+        when(index, all_copies[n].wait_recv)
+        copy = spread_share(index, n)
+        when(index, copy.start)
+        pair_copies.append((index, copy))
 
     grad_input = grad_input + jnp.concatenate(own_term, axis=1)
     for copy in term_copies:
         copy.wait_recv()
     for d in range(1, stripes):
-        grad_input = grad_input + term_buf[d].astype(F32)
+        grad_input = grad_input + term_buf[d, :edge].astype(F32)
+    bias_sum = jnp.concatenate(own_bias, axis=1)
+    for d in range(1, stripes):
+        bias_sum = bias_sum + term_buf[d, edge:].astype(F32)[:1]
+    gbias_ref[...] = bias_sum[0]
+    store_gbias.start()
     gin_ref[...] = grad_input
     store_gin.start()
 
-    for copy in grp_copies:
-        copy.wait_recv()
+    for index, copy in pair_copies:
+        when(index, copy.wait_recv)
     store_all.start()
+    for (d, x), copy in zip(others, chip_copies):
+        when(number(d, x), copy.wait_send)
+    for copy in all_copies:
+        when(me, copy.wait_send)
+    for index, copy in pair_copies:
+        when(index, copy.wait_send)
     for copy in pending:
         copy.wait_send()
     for store in stores:
@@ -355,10 +367,9 @@
         load.wait()
     for store in stores[2:]:
         store.start()
-    middle = all_ref.shape[0] // 2
-    gself_ref[...] = all_ref[:middle].reshape(gself_ref.shape).astype(F32)
+    gself_ref[...] = all_ref[0].astype(F32)
     stores[0].start()
-    gneigh_ref[...] = all_ref[middle:].reshape(gneigh_ref.shape).astype(F32)
+    gneigh_ref[...] = all_ref[1].astype(F32)
     stores[1].start()
     for store in stores:
         store.wait()
@@ -368,16 +379,16 @@
     stripes = lax.axis_size("stripe")
     reps = lax.axis_size("rep")
     edge, width = features.shape
-    chunk = 2 * self_weight.shape[0] // reps
-    sub = chunk // stripes if chunk % (PAD * stripes) == 0 else 0
-    share = (stripes, sub + PAD, width) if sub else (stripes, chunk + PAD, width)
+    chips = stripes * reps // CORES
+    depth = self_weight.shape[0]
+    owners = min(chips, depth // PAD)
+    rows = depth // owners
     hbm = pl.BlockSpec(memory_space=pl.ANY)
     dma = pltpu.SemaphoreType.DMA
     by_rep = [dma((reps,)), dma((reps,))]
-    by_stripe = [dma((stripes,)), dma((stripes,))]
     by_rep_half = [dma((reps, HALVES)), dma((reps, HALVES))]
     by_stripe_half = [dma((stripes, HALVES)), dma((stripes, HALVES))]
-    by_rep_stripe = [dma((reps, stripes)), dma((reps, stripes))]
+    by_chip = [dma((chips,)), dma((chips,))]
     out_shape = (
         jax.ShapeDtypeStruct((edge, width), BF16),
         jax.ShapeDtypeStruct((edge, width), F32),
@@ -385,10 +396,10 @@
         jax.ShapeDtypeStruct(neigh_weight.shape, F32),
         jax.ShapeDtypeStruct((width,), F32),
     )
-    shares = jax.ShapeDtypeStruct((reps, chunk, width), BF16)
+    shares = jax.ShapeDtypeStruct((CORES, depth, width), BF16)
     staged = (out_shape[0], out_shape[1], shares, out_shape[4])
     results = pl.pallas_call(
-        functools.partial(kernel, stripes, reps, sub),
+        functools.partial(kernel, stripes, reps, owners),
         out_shape=staged,
         in_specs=[hbm] * 8,
         out_specs=(hbm,) * 4,
@@ -409,18 +420,18 @@
             pltpu.VMEM((reps, edge, edge), BF16),
             pltpu.VMEM((reps, edge, width), BF16),
             pltpu.VMEM((reps, edge, width), BF16),
-            pltpu.VMEM((reps, edge, width), BF16),
-            pltpu.VMEM((stripes, edge, width), BF16),
-            pltpu.VMEM((stripes, edge, width), BF16),
-            pltpu.VMEM((reps, chunk + PAD, width), BF16),
-            pltpu.VMEM((reps, chunk + PAD, width), BF16),
-            pltpu.VMEM(share, BF16),
-            pltpu.VMEM(share, BF16),
+            pltpu.VMEM((reps, edge + PAD, width), BF16),
+            pltpu.VMEM((stripes, edge + PAD, width), BF16),
+            pltpu.VMEM((stripes, edge + PAD, width), BF16),
+            pltpu.VMEM((CORES, depth, width), BF16),
+            pltpu.VMEM((depth, width), BF16),
+            pltpu.VMEM((depth, width), BF16),
+            pltpu.VMEM((chips, rows, width), BF16),
             pltpu.VMEM((reps * edge, stripes * edge), BF16),
             pltpu.VMEM((stripes * edge, reps * edge), BF16),
         ]
         + by_stripe_half + by_rep + by_rep_half + by_rep_half + by_stripe_half
-        + by_rep + by_stripe + by_stripe + by_rep_stripe,
+        + [dma((1,)), dma((1,))] + by_chip + by_chip + by_chip,
         compiler_params=pltpu.CompilerParams(
             collective_id=0, has_side_effects=True, vmem_limit_bytes=60 * 2**20
         ),

time: 37.5 us -> 36 us (0.960)
  Pallas kernels: 36.7 us -> 35.2 us
    pallas_call x1, Pallas kernels: 34.7 us -> 33.2 us  [shards(): pl.pallas_call(functools.partial(kernel, stripes, reps, owners), out_shap...]
where the time goes in v3:
time: 36 us; the launch traced here: 35.8 us
  Pallas kernels  35.2 us (98%)
  between operations  0.64 us (2%)
    pallas_call x1, Pallas kernels, shards(): pl.pallas_call(functools.partial(kernel, stripes, reps, owners), out_shap...  33.2 us
    pallas_call x1, Pallas kernels, shards(): pl.pallas_call(finish, out_shape=out_shape, in_specs=[hbm] * 4, out_specs...  1.93 us

profile of v3, /device:TPU:0, one launch (start us, length us, event | category | flops | bytes accessed | tf_op | source)
XLA Modules:
  0.0 35.8 jit_solution(16560264073966550172)
XLA Ops:
  0.6 33.2 %shard_map.119 = (bf16[128,256]{1,0:T(8,128)(2,1)}, f32[128,256]{1,0:T(8,128)}, bf16[2,256,256]{2,1,0:T(8,128)(2,1)}, f32[256]{0:T(256)}) custom-call(s32[1,1,3]{2,1,0:T(1,128)} %row_hbm.1, s32[1,1,3]{2,1,0:T(1,128)} %src_hbm.1, bf16[128,256]{1,0:T(8,128)(2,1)} %feat_hbm.1, bf16[1,1,3,128,128]{4,3,2,1,0:T(8,128)(2,1)} %tiles_hbm.1, ...), custom_call_target="tpu_custom_call" | custom-call | tf_op jit(solution)/shard_map/pallas_call | solution.py:401
  33.9 1.9 %shard_map.120 = (bf16[128,256]{1,0:T(8,128)(2,1)}, f32[128,256]{1,0:T(8,128)}, f32[256,256]{1,0:T(8,128)}, f32[256,256]{1,0:T(8,128)}, f32[256]{0:T(256)}) custom-call(bf16[128,256]{1,0:T(8,128)(2,1)} %get-tuple-element.9.out_in, f32[128,256]{1,0:T(8,128)} %get-tuple-element.10.gin_in, bf16[2,256,256]{2,1,0:T(8,128)(2,1)} %get-tuple-element.11.all_in, ...), custom_call_target="tpu_custom_call" | custom-call | tf_op jit(solution)/shard_map/pallas_call | solution.py:439

commit v4 on v3

--- a/solution.py
+++ b/solution.py
@@ -82,6 +82,9 @@
     ]
     pending = []
 
+    for load in loads:
+        load.start()
+
     core = lax.rem(r, CORES)
     chips = reps // CORES
     others = [(d, x) for d in range(stripes) for x in range(chips)][1:]
@@ -103,8 +106,6 @@
     greeted = [to_chip(d, x) for d, x in others] + [to_rep(e) for e in range(1, reps, 2)]
     for device in greeted:
         pl.semaphore_signal(barrier, inc=1, device_id=device, device_id_type=MESH)
-    for load in loads:
-        load.start()
     load_feat.wait()
     pl.semaphore_wait(barrier, len(greeted))
 
@@ -202,12 +203,15 @@
     sigma = jax.nn.sigmoid(pre)
     slope = (cot_ref[...].astype(F32) * sigma * (1.0 + pre * (1.0 - sigma))).astype(BF16)
 
-    grads[0] = matmul(feats_t, slope).astype(BF16)
-    neigh_t = jnp.concatenate([n.astype(F32).T.astype(BF16) for n in neigh], axis=0)
-    grads[1] = matmul(neigh_t, slope).astype(BF16)
     core_copy = send(grads.at[1 - core], core_buf, (core_s, core_r), 0, partner)
-    core_copy.start()
-    pending.append(core_copy)
+
+    def weight_grads():
+        grads[0] = matmul(feats_t, slope).astype(BF16)
+        neigh_t = jnp.concatenate([n.astype(F32).T.astype(BF16) for n in neigh], axis=0)
+        grads[1] = matmul(neigh_t, slope).astype(BF16)
+        core_copy.start()
+        pending.append(core_copy)
+
     grad_bias = jnp.sum(slope.astype(F32), axis=0, keepdims=True)
     pull_buf[0, edge:] = jnp.broadcast_to(grad_bias, (PAD, width)).astype(BF16)
 
@@ -225,6 +229,8 @@
         for copy in pull_copies[h]:
             copy.start()
         pending += pull_copies[h]
+        if h == 0:
+            weight_grads()
 
     rows = grads.shape[1] // owners
     me = number(0, 0)

time: 36 us -> 35.7 us (level)
  no operation moved by 1% of the time
where the time goes in v4:
time: 35.7 us; the launch traced here: 35.6 us
  Pallas kernels  34.9 us (98%)
  between operations  0.64 us (2%)
    pallas_call x1, Pallas kernels, shards(): pl.pallas_call(functools.partial(kernel, stripes, reps, owners), out_shap...  33 us
    pallas_call x1, Pallas kernels, shards(): pl.pallas_call(finish, out_shape=out_shape, in_specs=[hbm] * 4, out_specs...  1.93 us

profile of v4, /device:TPU:0, one launch (start us, length us, event | category | flops | bytes accessed | tf_op | source)
XLA Modules:
  0.0 35.6 jit_solution(16640989126837906429)
XLA Ops:
  0.6 33.0 %shard_map.119 = (bf16[128,256]{1,0:T(8,128)(2,1)}, f32[128,256]{1,0:T(8,128)}, bf16[2,256,256]{2,1,0:T(8,128)(2,1)}, f32[256]{0:T(256)}) custom-call(s32[1,1,3]{2,1,0:T(1,128)} %row_hbm.1, s32[1,1,3]{2,1,0:T(1,128)} %src_hbm.1, bf16[128,256]{1,0:T(8,128)(2,1)} %feat_hbm.1, bf16[1,1,3,128,128]{4,3,2,1,0:T(8,128)(2,1)} %tiles_hbm.1, ...), custom_call_target="tpu_custom_call" | custom-call | tf_op jit(solution)/shard_map/pallas_call | solution.py:407
  33.7 1.9 %shard_map.120 = (bf16[128,256]{1,0:T(8,128)(2,1)}, f32[128,256]{1,0:T(8,128)}, f32[256,256]{1,0:T(8,128)}, f32[256,256]{1,0:T(8,128)}, f32[256]{0:T(256)}) custom-call(bf16[128,256]{1,0:T(8,128)(2,1)} %get-tuple-element.9.out_in, f32[128,256]{1,0:T(8,128)} %get-tuple-element.10.gin_in, bf16[2,256,256]{2,1,0:T(8,128)(2,1)} %get-tuple-element.11.all_in, ...), custom_call_target="tpu_custom_call" | custom-call | tf_op jit(solution)/shard_map/pallas_call | solution.py:445
